TPU v7x, 128 devices: a whole 4x4x4 slice. The times are simulated.
128 devices in a mesh: comp: 2 (over core), dom: 64 (over y, x, z).
Axes of the slice: x: 4, y: 4, z: 4, core: 2. Of those that a mesh axis runs over, the one named last changes fastest.
Arguments:
- model_state: float32 [2, 4, 16, 262144], P('comp', None, None, 'dom'), may hold values from -6 to 6
- neighbours: int32 [2, 8, 262144], P('comp', None, 'dom'), may hold values from 0 to 512, as said below
- stencil_coef: float32 [2, 8, 262144], P('comp', None, 'dom'), may hold values from 0.02 to 0.12
- column_mixing_operator: float32 [2, 16, 16], P('comp'), may hold values from -1.5 to 1.5
- remap_count: int32 [2, 64, 64], P('comp', 'dom'), may hold values from 256 to 1024, as said below
- remap_source: int32 [2, 64, 64, 1024], P('comp', 'dom'), may hold values from 0 to 4095
- remap_weight: float32 [2, 64, 64, 1024], P('comp', 'dom'), may hold values from 0.1 to 1
- remap_target: int32 [2, 64, 64, 1024], P('comp', 'dom'), may hold values from 0 to 4095
Outputs:
- updated_state: float32 [2, 4, 16, 262144], P('comp', None, None, 'dom')
- interface_flux_fields: float32 [2, 4, 262144], P('comp', None, 'dom')
Inputs may be any that keep to these rules, and one draw needn't show every extreme that they name: `neighbours`: in every partition's block some cell has an entry 0 and some an entry 512. remap_count[s, p, q] slots of partition p of section s go to partition q of the other section; every sender and every receiver has at least one pair with 1024 used slots.
All inputs are finite; a program needn't handle non-finite values.
Results may differ from a plain program's by a relative error of at most 0.0001.
Values sent between devices are 32-bit elements; how exact they have to be, the bound alone decides.
A program may use at most 256 MiB of HBM per device.

v0:
```python
import jax
import jax.numpy as jnp
from jax import lax
from jax.sharding import PartitionSpec as P


def padded(cells, sides, width):
    for axis, dim in sides:
        count = lax.axis_size(axis)
        head = lax.slice_in_dim(cells, 0, width, axis=dim)
        tail = lax.slice_in_dim(cells, cells.shape[dim] - width, cells.shape[dim], axis=dim)
        cells = jnp.concatenate(
            [
                lax.ppermute(tail, axis, [(i, (i + 1) % count) for i in range(count)]),
                cells,
                lax.ppermute(head, axis, [((i + 1) % count, i) for i in range(count)]),
            ],
            axis=dim,
        )
    return cells


def local(
    model_state,
    neighbours,
    stencil_coef,
    column_mixing_operator,
    remap_count,
    remap_source,
    remap_weight,
    remap_target,
):
    cells_dev = model_state.shape[3]
    field_count = model_state.shape[1]
    level_count = model_state.shape[2]
    stencil_size = neighbours.shape[1]
    peer_count = lax.axis_size("dom")
    margin = cells_dev // 16
    slot_count = remap_source.shape[3]
    domain_section = lax.axis_index("comp")
    export = model_state[0, :, 0, :]
    collected_flux = jnp.take(export, remap_source[0, 0].reshape(-1), axis=1).reshape(
        field_count, peer_count, slot_count
    )
    occupied = jnp.arange(slot_count, dtype=jnp.int32)[None, :] < remap_count[0, 0][:, None]
    weighted = jnp.where(
        occupied[None], remap_weight[0, 0][None] * collected_flux, jnp.zeros((), jnp.float32)
    )
    buffer = jnp.zeros((field_count, 2 * peer_count, slot_count), jnp.float32)
    buffer = lax.dynamic_update_slice_in_dim(buffer, weighted, (1 - domain_section) * peer_count, 1)
    arrived = lax.all_to_all(buffer, ("comp", "dom"), split_axis=1, concat_axis=1, tiled=True)
    received = lax.dynamic_slice_in_dim(arrived, (1 - domain_section) * peer_count, peer_count, 1)
    target_cells = remap_target[0, 0].reshape(-1)
    imported = (
        jnp.zeros((field_count, cells_dev), jnp.float32)
        .at[:, target_cells]
        .add(received.reshape(field_count, -1))
    )
    extended = padded(model_state, (("dom", 3),), margin)[0]
    row_count = field_count * level_count
    flat_extended = extended.reshape(row_count, -1)
    current = model_state[0]
    flat_current = current.reshape(row_count, cells_dev)
    cell_iota = jnp.arange(cells_dev, dtype=jnp.int32)
    lateral = jnp.zeros_like(flat_current)
    for neighbour in range(stencil_size):
        positions = cell_iota + neighbours[0, neighbour]
        adjacent = jnp.take(flat_extended, positions, axis=1)
        lateral = lateral + stencil_coef[0, neighbour][None, :] * (adjacent - flat_current)
    forcing_applied = current + lateral.reshape(field_count, level_count, cells_dev)
    forcing_applied = forcing_applied.at[:, 0, :].add(imported)
    advanced_state = jnp.einsum(
        "bx,exz->ebz", column_mixing_operator[0], forcing_applied, precision=lax.Precision.HIGHEST
    )
    return (advanced_state[None], imported[None])


def solution(mesh):
    in_specs = (
        P("comp", None, None, "dom"),
        P("comp", None, "dom"),
        P("comp", None, "dom"),
        P("comp", None, None),
        P("comp", "dom", None),
        P("comp", "dom", None, None),
        P("comp", "dom", None, None),
        P("comp", "dom", None, None),
    )
    out_specs = (P("comp", None, None, "dom"), P("comp", None, "dom"))
    return jax.shard_map(local, mesh=mesh, in_specs=in_specs, out_specs=out_specs, check_vma=False)
```

profile of v0, /device:TPU:1, one launch (start us, length us, event | category | flops | bytes accessed | tf_op | source)
XLA Modules:
  0.0 880.6 jit_solution(10094863659682813926)
XLA Ops:
  4.6 6.8 collective-permute-start.1
  11.4 17.0 %copy.86 = f32[1,4,16,4096]{1,3,2,0:T(8,128)} copy(f32[1,4,16,4096]{3,2,1,0:T(8,128)} %param.12) | data formatting | bytes 2097152 | tf_op args[0]
  30.8 215.9 %gather_fusion = f32[65536,4]{1,0:T(8,128)} fusion(f32[4,4096]{0,1:T(8,128)S(1)} %slice_bitcast_fusion, s32[65536]{0:T(1024)S(1)} %broadcast_clamp_fusion), kind=kCustom, calls=%fused_computation.8 | custom fusion | bytes 2359296 | tf_op jit(solution)/shard_map/jit(_take)/gather | solution.py:42
  246.7 17.6 %copy.105 = f32[4,64,1024]{2,0,1:T(4,128)S(1)} copy(f32[4,64,1024]{0,2,1:T(8,128)} %bitcast.119) | data formatting | bytes 2097152 | tf_op jit(solution)/shard_map/jit(_take)/gather | solution.py:42
  268.0 5.6 all-to-all-start
  285.6 15.4 %gather_fusion.7 = f32[4096,64]{1,0:T(8,128)} fusion(f32[64,4608]{0,1:T(8,128)S(1)} %copy.87, s32[4096]{0:T(1024)} %fusion.24), kind=kCustom, calls=%fused_computation.6.clone | custom fusion | bytes 2113536 | tf_op jit(solution)/shard_map/jit(_take)/gather | solution.py:68
  304.2 15.4 %gather_fusion.8 = f32[4096,64]{1,0:T(8,128)} fusion(f32[64,4608]{0,1:T(8,128)S(1)} %copy.87, s32[4096]{0:T(1024)} %fusion.25), kind=kCustom, calls=%fused_computation.7.clone | custom fusion | bytes 2113536 | tf_op jit(solution)/shard_map/jit(_take)/gather | solution.py:68
  322.8 15.4 %gather_fusion.1 = f32[4096,64]{1,0:T(8,128)} fusion(f32[64,4608]{0,1:T(8,128)S(1)} %copy.87, s32[4096]{0:T(1024)} %fusion.18), kind=kCustom, calls=%fused_computation.clone | custom fusion | bytes 2113536 | tf_op jit(solution)/shard_map/jit(_take)/gather | solution.py:68
  338.2 3.2 copy.88
  341.4 15.4 %gather_fusion.2 = f32[4096,64]{1,0:T(8,128)} fusion(f32[64,4608]{0,1:T(8,128)S(1)} %copy.87, s32[4096]{0:T(1024)} %fusion.19), kind=kCustom, calls=%fused_computation.1.clone | custom fusion | bytes 2113536 | tf_op jit(solution)/shard_map/jit(_take)/gather | solution.py:68
  356.8 3.2 copy.90
  360.0 15.4 %gather_fusion.3 = f32[4096,64]{1,0:T(8,128)} fusion(f32[64,4608]{0,1:T(8,128)S(1)} %copy.87, s32[4096]{0:T(1024)} %fusion.20), kind=kCustom, calls=%fused_computation.2.clone | custom fusion | bytes 2113536 | tf_op jit(solution)/shard_map/jit(_take)/gather | solution.py:68
  378.5 15.4 %gather_fusion.4 = f32[4096,64]{1,0:T(8,128)} fusion(f32[64,4608]{0,1:T(8,128)S(1)} %copy.87, s32[4096]{0:T(1024)} %fusion.21), kind=kCustom, calls=%fused_computation.3.clone | custom fusion | bytes 2113536 | tf_op jit(solution)/shard_map/jit(_take)/gather | solution.py:68
  397.1 15.4 %gather_fusion.5 = f32[4096,64]{1,0:T(8,128)} fusion(f32[64,4608]{0,1:T(8,128)S(1)} %copy.87, s32[4096]{0:T(1024)} %fusion.22), kind=kCustom, calls=%fused_computation.4.clone | custom fusion | bytes 2113536 | tf_op jit(solution)/shard_map/jit(_take)/gather | solution.py:68
  412.5 3.2 copy.96
  415.8 15.4 %gather_fusion.6 = f32[4096,64]{1,0:T(8,128)} fusion(f32[64,4608]{0,1:T(8,128)S(1)} %copy.87, s32[4096]{0:T(1024)} %fusion.23), kind=kCustom, calls=%fused_computation.5.clone | custom fusion | bytes 2113536 | tf_op jit(solution)/shard_map/jit(_take)/gather | solution.py:68
  431.2 3.3 copy.98
  434.6 5.2 fusion.2
  439.8 17.0 %copy.103 = f32[4,16,4096]{0,2,1:T(8,128)} copy(f32[4,16,4096]{2,1,0:T(8,128)} %bitcast.123) | data formatting | bytes 2097152 | tf_op jit(solution)/shard_map/reshape | solution.py:70
  456.8 33.3 %bitcast_add_fusion = f32[4,16,4096]{0,2,1:T(8,128)} fusion(f32[4,16,4096]{0,2,1:T(8,128)} %copy.103, f32[1,4,16,4096]{1,3,2,0:T(8,128)} %copy.86), kind=kLoop, calls=%fused_computation.10 | loop fusion | flops 262144 | bytes 3145728 | tf_op jit(solution)/shard_map/add | solution.py:70
  491.4 16.0 %copy.106 = f32[65536,4]{1,0:T(8,128)} copy(f32[65536,4]{0,1:T(4,128)S(1)} %bitcast.122) | data formatting | bytes 2097152 | tf_op jit(solution)/shard_map/reshape | solution.py:57
  507.4 347.8 %scatter_custom_fusion = f32[4,4096]{0,1:T(8,128)S(1)} fusion(s32[65536]{0:T(1024)} %bitcast.127, f32[65536,4]{1,0:T(8,128)} %copy.106, f32[]{:T(128)} %constant.61.clone.1), kind=kCustom, calls=%fused_computation.42 | custom fusion | flops 262144 | bytes 66048 | tf_op jit(solution)/shard_map/scatter-add | solution.py:57
  855.3 3.3 fusion
  858.6 18.8 %copy.107 = f32[4,16,4096]{2,1,0:T(8,128)S(1)} copy(f32[4,16,4096]{0,2,1:T(8,128)} %fusion) | data formatting | bytes 2097152 | tf_op jit(solution)/shard_map/scatter-add | solution.py:71
  (69 shorter events, 39.1 us)
Async XLA Ops:
  0.6 878.0 %copy-start = (f32[1,16,16]{2,1,0:T(8,128)S(1)}, f32[1,16,16]{2,1,0:T(8,128)}, u32[]{:S(2)}) copy-start(f32[1,16,16]{2,1,0:T(8,128)} %param.15) | copy-start | bytes 3076
  2.2 279.6 %collective-permute-start = (f32[1,4,16,256]{3,2,1,0:T(8,128)}, f32[1,4,16,256]{3,2,1,0:T(8,128)}, u32[]{:S(2)}, u32[]{:S(2)}) collective-permute-start(f32[1,4,16,256]{3,2,1,0:T(8,128)} %get-tuple-element.25), channel_id=1, source_target_pairs={{0,1},{1,2},{2,3},{3,4},{4,5},{5,6},{6,7},{7,8},{8,9},{9,10},{10,1... | collective-permute-start | bytes 196616 | tf_op jit(solution)/shard_map/ppermute | solution.py:14
  4.6 277.2 %collective-permute-start.1 = (f32[1,4,16,256]{3,2,1,0:T(8,128)}, f32[1,4,16,256]{3,2,1,0:T(8,128)}, u32[]{:S(2)}, u32[]{:S(2)}) collective-permute-start(f32[1,4,16,256]{3,2,1,0:T(8,128)} %get-tuple-element.26), channel_id=1, source_target_pairs={{1,0},{2,1},{3,2},{4,3},{5,4},{6,5},{7,6},{8,7},{9,8},{10,9},{11,1... | collective-permute-start | bytes 196616 | tf_op jit(solution)/shard_map/ppermute | solution.py:16
  28.4 1.8 copy-start.4
  246.7 17.6 %copy-start.15 = (s32[1,1,64]{2,1,0:T(1,128)S(1)}, s32[1,1,64]{2,1,0:T(1,128)}, u32[]{:S(2)}) copy-start(s32[1,1,64]{2,1,0:T(1,128)} %param.16) | copy-start | bytes 772
  264.3 2.0 copy-start.6
  268.0 5.6 copy-start.7
  268.0 11.8 %copy-start.8 = (f32[1,8,4096]{2,1,0:T(8,128)S(1)}, f32[1,8,4096]{2,1,0:T(8,128)}, u32[]{:S(2)}) copy-start(f32[1,8,4096]{2,1,0:T(8,128)} %param.14) | copy-start | bytes 393220
  268.0 11.9 %copy-start.5 = (s32[1,1,64,1024]{3,2,1,0:T(8,128)S(1)}, s32[1,1,64,1024]{3,2,1,0:T(8,128)}, u32[]{:S(2)}) copy-start(s32[1,1,64,1024]{3,2,1,0:T(8,128)} %param.19) | copy-start | bytes 786436
  268.0 13.8 %copy-start.1 = (f32[1,4,16,4096]{3,2,1,0:T(8,128)S(1)}, f32[1,4,16,4096]{3,2,1,0:T(8,128)}, u32[]{:S(2)}) copy-start(f32[1,4,16,4096]{3,2,1,0:T(8,128)} %param.12) | copy-start | bytes 3145732
  268.0 222.1 %all-to-all-start = ((f32[4,128,1024]{2,0,1:T(4,128)}), f32[4,128,1024]{2,0,1:T(4,128)}, u32[]{:S(2)}, u32[]{:S(2)}) async-start(f32[4,128,1024]{2,0,1:T(4,128)} %select_dynamic-update-slice_fusion), calls=%async_computation | async-start | bytes 4194304 | tf_op jit(solution)/shard_map/all_to_all | solution.py:51
  431.2 3.4 copy-start.2
  431.2 3.4 copy-start.3
  431.2 3.4 copy-start.9
  431.2 3.4 copy-start.10
  431.2 3.4 copy-start.11
  431.2 3.4 copy-start.12
  431.2 3.4 copy-start.13
  431.2 3.4 copy-start.14
where the time goes:
time: 885 us; the launch traced here: 881 us
  local copies, waits for them, and re-layouts  461 us (52%)
  other arithmetic  401 us (45%)
  starting transfers between devices  14.8 us (2%)
    scatter-add x1, other arithmetic, local(): imported = jnp.zeros((field_count, cells_dev), jnp.float32).at[:, target_...  348 us
    gather x2, local copies, waits for them, and re-layouts, local(): jnp.take(export, remap_source[0, 0].reshape(-1), axis=1)  234 us
    gather x16, local copies, waits for them, and re-layouts, local(): adjacent = jnp.take(flat_extended, positions, axis=1)  149 us
    add x1, other arithmetic, local(): current + lateral.reshape(field_count, level_count, cells_dev)  33.3 us
    unnamed x36, local copies, waits for them, and re-layouts  18.9 us
    scatter-add x1, local copies, waits for them, and re-layouts, local(): forcing_applied = forcing_applied.at[:, 0, :].add(imported)  18.8 us
  transfers between devices with their start and end apart: 3, of which 0 were waited for; matrix products, arithmetic and copies ran while one was open for 54% of the time, Pallas kernels for 0%

commit v1 on v0

v1 whole, which is shorter than its diff:
```python
import functools

import jax
import jax.numpy as jnp
from jax import lax
from jax.experimental import pallas as pl
from jax.experimental.pallas import tpu as pltpu
from jax.sharding import PartitionSpec as P

MESH = pl.DeviceIdType.MESH
F32, BF16, I32, I16 = jnp.float32, jnp.bfloat16, jnp.int32, jnp.int16
LANES = 128
SIDE = 4
PEERS = SIDE**3
VARS, LEV, NBR = 4, 16, 8
CELLS = 4096
CAP = 1024
HALO = 256
BLOCKS = CELLS // LANES
CHUNKS = CAP // LANES
ROWS = VARS * LEV
FROM_LEFT, FROM_RIGHT = 0, HALO + CELLS


def halves(x):
    high = x.astype(BF16)
    return high, (x - high.astype(F32)).astype(BF16)


def lane_pick(table, index):
    return jnp.take_along_axis(table, index, axis=1, mode="promise_in_bounds")


def sublane_pick(table, index):
    return jnp.take_along_axis(table, index, axis=0, mode="promise_in_bounds")


def peer_at(me, step, sign):
    place = 0
    for unit in (16, 4, 1):
        at = lax.rem(lax.div(me, unit), SIDE)
        move = lax.rem(lax.div(step, unit), SIDE)
        place = place + unit * lax.rem(at + sign * move + SIDE, SIDE)
    return place


def kernel(
    state_hbm,
    neighbours_hbm,
    coef_hbm,
    mixing_ref,
    count_ref,
    source_hbm,
    weight_hbm,
    target_hbm,
    mixed_hbm,
    flux_ref,
    ext,
    nbr,
    coef,
    raw_source,
    raw_weight,
    raw_target,
    source,
    weight,
    target,
    table,
    sendbuf,
    recvbuf,
    mixed,
    total,
    in_sems,
    halo_send_sems,
    halo_recv_sems,
    send_sems,
    recv_sems,
    out_sem,
):
    comp, me = lax.axis_index("comp"), lax.axis_index("dom")
    other = 1 - comp
    right, left = lax.rem(me + 1, PEERS), lax.rem(me + PEERS - 1, PEERS)

    loads = [
        pltpu.make_async_copy(src, dst, in_sems.at[i])
        for i, (src, dst) in enumerate(
            (
                (state_hbm.at[0], ext.at[:, :, pl.ds(HALO, CELLS)]),
                (source_hbm.at[0, 0], raw_source),
                (weight_hbm.at[0, 0], raw_weight),
                (neighbours_hbm.at[0], nbr),
                (coef_hbm.at[0], coef),
                (target_hbm.at[0, 0], raw_target),
            )
        )
    ]
    for load in loads:
        load.start()

    barrier = pltpu.get_barrier_semaphore()

    def greet(step, c):
        pl.semaphore_signal(barrier, inc=1, device_id=(other, step), device_id_type=MESH)
        return c

    lax.fori_loop(0, PEERS, greet, 0)
    for side in (left, right):
        pl.semaphore_signal(barrier, inc=1, device_id=(comp, side), device_id_type=MESH)

    loads[0].wait()
    for v in range(VARS):
        for b in range(BLOCKS):
            table[v * BLOCKS + b : v * BLOCKS + b + 1, :] = ext[
                v, 0:1, HALO + b * LANES : HALO + (b + 1) * LANES
            ]
    table_halves = jnp.concatenate(halves(table[...]), axis=1)

    loads[1].wait()
    loads[2].wait()

    def by_peer(raw, tidy):
        for g in range(PEERS // 8):
            for c in range(CHUNKS):
                tidy[pl.ds(g * 8 * CHUNKS + c, 8, stride=CHUNKS), :] = raw[
                    g * 8 : g * 8 + 8, c * LANES : (c + 1) * LANES
                ]

    by_peer(raw_source, source)
    by_peer(raw_weight, weight)

    pl.semaphore_wait(barrier, PEERS + 2)

    halos = [
        pltpu.make_async_remote_copy(
            src_ref=state_hbm.at[0, :, :, pl.ds(start, HALO)],
            dst_ref=ext.at[:, :, pl.ds(place, HALO)],
            send_sem=halo_send_sems.at[i],
            recv_sem=halo_recv_sems.at[i],
            device_id=(comp, side),
            device_id_type=MESH,
        )
        for i, (start, place, side) in enumerate(
            ((CELLS - HALO, FROM_LEFT, right), (0, FROM_RIGHT, left))
        )
    ]
    for halo in halos:
        halo.start()

    sublane = lax.broadcasted_iota(I32, (8, LANES), 0)
    lane = lax.broadcasted_iota(I32, (8, LANES), 1)
    slot = sublane * LANES + lane
    lane_rows = lax.broadcasted_iota(I32, (LANES, 1), 0).astype(I16)
    block_rows = lax.broadcasted_iota(I32, (BLOCKS, 1), 0).astype(I16)
    one, nought = BF16(1), BF16(0)

    def to_peer(q):
        return pltpu.make_async_remote_copy(
            src_ref=sendbuf.at[q],
            dst_ref=recvbuf.at[me],
            send_sem=send_sems.at[q],
            recv_sem=recv_sems.at[me],
            device_id=(other, q),
            device_id_type=MESH,
        )

    def from_peer(p):
        return pltpu.make_async_remote_copy(
            src_ref=sendbuf.at[p],
            dst_ref=recvbuf.at[p],
            send_sem=send_sems.at[p],
            recv_sem=recv_sems.at[p],
            device_id=(other, p),
            device_id_type=MESH,
        )

    def gather(step, c_):
        q = peer_at(me, step, 1)
        cells = source[pl.ds(pl.multiple_of(q * CHUNKS, CHUNKS), CHUNKS), :]
        low, high = cells & (LANES - 1), cells >> 7
        used = jnp.where(
            slot < count_ref[0, 0, q],
            weight[pl.ds(pl.multiple_of(q * CHUNKS, CHUNKS), CHUNKS), :],
            0.0,
        )
        out = [jnp.zeros((8, LANES), F32) for _ in range(VARS)]
        for n in range(CHUNKS // 2):
            lows = jnp.concatenate([low[2 * n : 2 * n + 1], low[2 * n + 1 : 2 * n + 2]], axis=1)
            hot = jnp.where(lane_rows == lows.astype(I16), one, nought)
            rows = jnp.dot(
                table_halves,
                jnp.concatenate([hot, hot], axis=0),
                preferred_element_type=F32,
            )
            for half in range(2):
                c = 2 * n + half
                row = jnp.broadcast_to(high[c : c + 1], (8, LANES))
                within, group = row & 7, row >> 3
                for v in range(VARS):
                    picks = [
                        sublane_pick(
                            rows[
                                v * BLOCKS + t * 8 : v * BLOCKS + t * 8 + 8,
                                half * LANES : (half + 1) * LANES,
                            ],
                            within,
                        )
                        for t in range(BLOCKS // 8)
                    ]
                    pick = jnp.where(
                        group < 2,
                        jnp.where(group == 0, picks[0], picks[1]),
                        jnp.where(group == 2, picks[2], picks[3]),
                    )
                    out[v] = jnp.where(sublane == c, pick, out[v])
        for v in range(VARS):
            sendbuf[q, v * 8 : v * 8 + 8, :] = out[v] * used
        to_peer(q).start()
        return c_

    lax.fori_loop(0, PEERS, gather, 0)

    spread = (
        lax.rem(lax.broadcasted_iota(I32, (ROWS, LEV), 0), LEV)
        == lax.broadcasted_iota(I32, (ROWS, LEV), 1)
    ).astype(F32)
    tiled = lax.dot_general(
        jnp.dot(spread, mixing_ref[0], precision=lax.Precision.HIGHEST, preferred_element_type=F32),
        spread,
        (((1,), (1,)), ((), ())),
        precision=lax.Precision.HIGHEST,
        preferred_element_type=F32,
    )
    same = lax.div(lax.broadcasted_iota(I32, (ROWS, ROWS), 0), LEV) == lax.div(
        lax.broadcasted_iota(I32, (ROWS, ROWS), 1), LEV
    )
    mix_high, mix_low = halves(jnp.where(same, tiled, 0.0))
    mix_high = jnp.concatenate([mix_high, mix_high], axis=1)
    mix_low = jnp.concatenate([mix_low, mix_low], axis=1)

    loads[3].wait()
    loads[4].wait()
    for halo in halos:
        halo.wait_recv()

    def stencil(b, c_):
        base = pl.multiple_of(b * LANES, LANES)
        near = nbr[:, pl.ds(base, LANES)]
        coefs = coef[:, pl.ds(base, LANES)]

        def rows(r, s):
            return ext[r // 2, (r % 2) * 8 : (r % 2) * 8 + 8, pl.ds(base + s * LANES, LANES)]

        now = [rows(r, 2) for r in range(ROWS // 8)]
        acc = list(now)
        for j in range(NBR):
            place = lane + near[j : j + 1]
            at, block = place & (LANES - 1), place >> 7
            factor = jnp.broadcast_to(coefs[j : j + 1], (8, LANES))
            for r in range(ROWS // 8):
                pick = lane_pick(rows(r, 0), at)
                for s in range(1, 5):
                    pick = jnp.where(block == s, lane_pick(rows(r, s), at), pick)
                acc[r] = acc[r] + factor * (pick - now[r])
        high, low = halves(jnp.concatenate(acc, axis=0))
        both = jnp.concatenate([high, low], axis=0)
        result = jnp.dot(mix_high, both, preferred_element_type=F32) + jnp.dot(
            mix_low, both, preferred_element_type=F32
        )
        for v in range(VARS):
            mixed[v, :, pl.ds(base, LANES)] = result[v * LEV : (v + 1) * LEV]
        return c_

    lax.fori_loop(0, BLOCKS, stencil, 0)
    store = pltpu.make_async_copy(mixed, mixed_hbm, out_sem)
    store.start()

    loads[5].wait()
    by_peer(raw_target, target)
    total[...] = jnp.zeros_like(total)

    def scatter(step, c_):
        p = peer_at(me, step, -1)
        from_peer(p).wait_recv()
        cells = target[pl.ds(pl.multiple_of(p * CHUNKS, CHUNKS), CHUNKS), :]
        low, high = (cells & (LANES - 1)), (cells >> 7)
        values, hots = [], []
        for c in range(CHUNKS):
            here = block_rows == high[c : c + 1].astype(I16)
            hots.append(jnp.where(lane_rows == low[c : c + 1].astype(I16), one, nought))
            parts = [halves(recvbuf[p, v * 8 + c : v * 8 + c + 1, :]) for v in range(VARS)]
            values.append(
                jnp.concatenate(
                    [jnp.where(here, parts[v][i], nought) for i in range(2) for v in range(VARS)],
                    axis=0,
                )
            )
        total[...] += lax.dot_general(
            jnp.concatenate(values, axis=1),
            jnp.concatenate(hots, axis=1),
            (((1,), (1,)), ((), ())),
            preferred_element_type=F32,
        )
        return c_

    lax.fori_loop(0, PEERS, scatter, 0)

    for v in range(VARS):
        for b in range(BLOCKS):
            r = v * BLOCKS + b
            flux_ref[v : v + 1, b * LANES : (b + 1) * LANES] = (
                total[r : r + 1, :] + total[r + VARS * BLOCKS : r + VARS * BLOCKS + 1, :]
            )

    def sent(step, c_):
        to_peer(step).wait_send()
        return c_

    lax.fori_loop(0, PEERS, sent, 0)
    for halo in halos:
        halo.wait_send()
    store.wait()


def local(
    model_state,
    neighbours,
    stencil_coef,
    column_mixing_operator,
    remap_count,
    remap_source,
    remap_weight,
    remap_target,
):
    hbm = pl.BlockSpec(memory_space=pltpu.HBM)
    vmem = pl.BlockSpec(memory_space=pltpu.VMEM)
    smem = pl.BlockSpec(memory_space=pltpu.SMEM)
    mixed, flux = pl.pallas_call(
        kernel,
        out_shape=(
            jax.ShapeDtypeStruct((VARS, LEV, CELLS), F32),
            jax.ShapeDtypeStruct((VARS, CELLS), F32),
        ),
        in_specs=[hbm, hbm, hbm, vmem, smem, hbm, hbm, hbm],
        out_specs=(hbm, vmem),
        scratch_shapes=[
            pltpu.VMEM((VARS, LEV, CELLS + 2 * HALO), F32),
            pltpu.VMEM((NBR, CELLS), I32),
            pltpu.VMEM((NBR, CELLS), F32),
            pltpu.VMEM((PEERS, CAP), I32),
            pltpu.VMEM((PEERS, CAP), F32),
            pltpu.VMEM((PEERS, CAP), I32),
            pltpu.VMEM((PEERS * CHUNKS, LANES), I32),
            pltpu.VMEM((PEERS * CHUNKS, LANES), F32),
            pltpu.VMEM((PEERS * CHUNKS, LANES), I32),
            pltpu.VMEM((VARS * BLOCKS, LANES), F32),
            pltpu.VMEM((PEERS, VARS * CHUNKS, LANES), F32),
            pltpu.VMEM((PEERS, VARS * CHUNKS, LANES), F32),
            pltpu.VMEM((VARS, LEV, CELLS), F32),
            pltpu.VMEM((2 * VARS * BLOCKS, LANES), F32),
            pltpu.SemaphoreType.DMA((6,)),
            pltpu.SemaphoreType.DMA((2,)),
            pltpu.SemaphoreType.DMA((2,)),
            pltpu.SemaphoreType.DMA((PEERS,)),
            pltpu.SemaphoreType.DMA((PEERS,)),
            pltpu.SemaphoreType.DMA,
        ],
        compiler_params=pltpu.CompilerParams(
            collective_id=0, has_side_effects=True, vmem_limit_bytes=32 << 20
        ),
        name="step",
    )(
        model_state,
        neighbours,
        stencil_coef,
        column_mixing_operator,
        remap_count,
        remap_source,
        remap_weight,
        remap_target,
    )
    updated = mixed + column_mixing_operator[0, :, 0][None, :, None] * flux[:, None, :]
    return updated[None], flux[None]


def solution(mesh):
    in_specs = (
        P("comp", None, None, "dom"),
        P("comp", None, "dom"),
        P("comp", None, "dom"),
        P("comp", None, None),
        P("comp", "dom", None),
        P("comp", "dom", None, None),
        P("comp", "dom", None, None),
        P("comp", "dom", None, None),
    )
    out_specs = (P("comp", None, None, "dom"), P("comp", None, "dom"))
    return jax.shard_map(local, mesh=mesh, in_specs=in_specs, out_specs=out_specs, check_vma=False)
```

time: 885 us -> 81.3 us (0.09)
  local copies, waits for them, and re-layouts: 461 us -> 7.38 us
  other arithmetic: 401 us -> 1.13 us
  Pallas kernels: 0 us -> 71.8 us
  starting transfers between devices: 14.8 us -> 0 us
    gather x18 -> x0, local copies, waits for them, and re-layouts: 382 us -> none  [the longest x2 234 us: local(): jnp.take(export, remap_source[0, 0].reshape(-1), axis=1)]
    scatter-add x2 -> x0, other arithmetic: 351 us -> none  [the longest x1 348 us: local(): imported = jnp.zeros((field_count, cells_dev), jnp.float32).at[:, target_...]
    pallas_call x0 -> x1, Pallas kernels: none -> 71.8 us  [local(): pl.pallas_call(kernel, out_shape=(jax.ShapeDtypeStruct((VARS, LEV, CELLS)...]
    add x2 -> x0, other arithmetic: 38.5 us -> none  [the longest x1 33.3 us: local(): current + lateral.reshape(field_count, level_count, cells_dev)]
    reshape x2 -> x0, local copies, waits for them, and re-layouts: 33 us -> none  [the longest x1 17 us: local(): lateral.reshape(field_count, level_count, cells_dev)]
    scatter-add x1 -> x0, local copies, waits for them, and re-layouts: 18.8 us -> none  [local(): forcing_applied = forcing_applied.at[:, 0, :].add(imported)]
    unnamed x36 -> x17, local copies, waits for them, and re-layouts: 18.9 us -> 6.51 us
    ppermute x2 -> x0, starting transfers between devices: 9.23 us -> none  [the longest x1 6.77 us: padded(): lax.ppermute(head, axis, [((i + 1) % count, i) for i in range(count)])]
  transfers between devices with their start and end apart: 3 -> 0, of which waited for: 0 -> 0; matrix products, arithmetic and copies ran while one was open for 54% -> 0% of each run, Pallas kernels for 0% -> 0%
where the time goes in v1:
time: 81.3 us; the launch traced here: 81 us
  Pallas kernels  71.8 us (88%)
  local copies, waits for them, and re-layouts  7.38 us (9%)
  other arithmetic  1.13 us (1%)
    pallas_call x1, Pallas kernels, local(): pl.pallas_call(kernel, out_shape=(jax.ShapeDtypeStruct((VARS, LEV, CELLS)...  71.8 us
    unnamed x17, local copies, waits for them, and re-layouts  6.51 us

profile of v1, /device:TPU:1, one launch (start us, length us, event | category | flops | bytes accessed | tf_op | source)
XLA Modules:
  0.0 81.0 jit_solution(7752516519236775424)
XLA Ops:
  0.6 0.0 copy-start.6
  0.6 0.0 copy-start.7
  0.6 0.9 %slice_reduce_fusion = f32[16]{0:T(128)S(1)} fusion(f32[1,16,16]{2,1,0:T(8,128)} %mixing_ref.1), kind=kLoop, calls=%fused_computation.1 | loop fusion | bytes 128 | tf_op jit(solution)/shard_map/slice | solution.py:380
  1.5 0.0 copy-done.6
  1.5 0.0 copy-done.7
  1.5 0.0 copy-start
  1.5 1.2 %copy-done = f32[1,4,16,4096]{3,2,1,0:T(8,128)S(1)} copy-done((f32[1,4,16,4096]{3,2,1,0:T(8,128)S(1)}, f32[1,4,16,4096]{3,2,1,0:T(8,128)}, u32[]{:S(2)}) %copy-start) | copy-done | bytes 1048600
  2.8 0.0 copy-start.1
  2.8 0.9 %copy-done.1 = s32[1,1,64,1024]{3,2,1,0:T(8,128)S(1)} copy-done((s32[1,1,64,1024]{3,2,1,0:T(8,128)S(1)}, s32[1,1,64,1024]{3,2,1,0:T(8,128)}, u32[]{:S(2)}) %copy-start.1) | copy-done | bytes 262168
  3.7 0.0 copy-start.2
  3.7 0.9 %copy-done.2 = f32[1,1,64,1024]{3,2,1,0:T(8,128)S(1)} copy-done((f32[1,1,64,1024]{3,2,1,0:T(8,128)S(1)}, f32[1,1,64,1024]{3,2,1,0:T(8,128)}, u32[]{:S(2)}) %copy-start.2) | copy-done | bytes 262168
  4.7 0.0 copy-start.3
  4.7 0.9 %copy-done.3 = s32[1,1,64,1024]{3,2,1,0:T(8,128)S(1)} copy-done((s32[1,1,64,1024]{3,2,1,0:T(8,128)S(1)}, s32[1,1,64,1024]{3,2,1,0:T(8,128)}, u32[]{:S(2)}) %copy-start.3) | copy-done | bytes 262168
  5.6 0.0 copy-start.4
  5.6 0.9 %copy-done.4 = s32[1,8,4096]{2,1,0:T(8,128)S(1)} copy-done((s32[1,8,4096]{2,1,0:T(8,128)S(1)}, s32[1,8,4096]{2,1,0:T(8,128)}, u32[]{:S(2)}) %copy-start.4) | copy-done | bytes 131096
  6.5 0.0 copy-start.5
  6.5 0.9 %copy-done.5 = f32[1,8,4096]{2,1,0:T(8,128)S(1)} copy-done((f32[1,8,4096]{2,1,0:T(8,128)S(1)}, f32[1,8,4096]{2,1,0:T(8,128)}, u32[]{:S(2)}) %copy-start.5) | copy-done | bytes 131096
  7.4 71.8 %step.1 = (f32[4,16,4096]{2,1,0:T(8,128)S(1)}, f32[4,4096]{1,0:T(4,128)S(1)}) custom-call(f32[1,4,16,4096]{3,2,1,0:T(8,128)S(1)} %copy-done, s32[1,8,4096]{2,1,0:T(8,128)S(1)} %copy-done.4, f32[1,8,4096]{2,1,0:T(8,128)S(1)} %copy-done.5, f32[1,16,16]{2,1,0:T(8,128)S(1)} %copy-done.6, s32[1,1,64]{2,1,0:T(1,128)S(1)} %copy-done.7, ...), custom_call_target="tpu_custom_call" | custom-call | tf_op jit(solution)/shard_map/step/pallas_call | solution.py:336
  79.2 1.1 %add_bitcast_fusion = f32[1,4,16,4096]{3,2,1,0:T(8,128)} fusion(f32[4,16,4096]{2,1,0:T(8,128)S(1)} %get-tuple-element.4, f32[4,4096]{1,0:T(4,128)S(1)} %get-tuple-element.5, f32[16]{0:T(128)S(1)} %slice_reduce_fusion), kind=kLoop, calls=%fused_computation | loop fusion | flops 524288 | bytes 2162752 | tf_op jit(solution)/shard_map/broadcast_in_dim | solution.py:381
  80.3 0.6 copy.11
Async XLA Ops:
  0.6 0.9 %copy-start.6 = (f32[1,16,16]{2,1,0:T(8,128)S(1)}, f32[1,16,16]{2,1,0:T(8,128)}, u32[]{:S(2)}) copy-start(f32[1,16,16]{2,1,0:T(8,128)} %mixing_ref.1) | copy-start | bytes 3076
  0.6 0.9 %copy-start.7 = (s32[1,1,64]{2,1,0:T(1,128)S(1)}, s32[1,1,64]{2,1,0:T(1,128)}, u32[]{:S(2)}) copy-start(s32[1,1,64]{2,1,0:T(1,128)} %count_ref.1) | copy-start | bytes 772
  1.5 1.2 %copy-start = (f32[1,4,16,4096]{3,2,1,0:T(8,128)S(1)}, f32[1,4,16,4096]{3,2,1,0:T(8,128)}, u32[]{:S(2)}) copy-start(f32[1,4,16,4096]{3,2,1,0:T(8,128)} %state_hbm.1) | copy-start | bytes 3145732
  2.8 0.9 %copy-start.1 = (s32[1,1,64,1024]{3,2,1,0:T(8,128)S(1)}, s32[1,1,64,1024]{3,2,1,0:T(8,128)}, u32[]{:S(2)}) copy-start(s32[1,1,64,1024]{3,2,1,0:T(8,128)} %source_hbm.1) | copy-start | bytes 786436
  3.7 0.9 %copy-start.2 = (f32[1,1,64,1024]{3,2,1,0:T(8,128)S(1)}, f32[1,1,64,1024]{3,2,1,0:T(8,128)}, u32[]{:S(2)}) copy-start(f32[1,1,64,1024]{3,2,1,0:T(8,128)} %weight_hbm.1) | copy-start | bytes 786436
  4.7 0.9 %copy-start.3 = (s32[1,1,64,1024]{3,2,1,0:T(8,128)S(1)}, s32[1,1,64,1024]{3,2,1,0:T(8,128)}, u32[]{:S(2)}) copy-start(s32[1,1,64,1024]{3,2,1,0:T(8,128)} %target_hbm.1) | copy-start | bytes 786436
  5.6 0.9 %copy-start.4 = (s32[1,8,4096]{2,1,0:T(8,128)S(1)}, s32[1,8,4096]{2,1,0:T(8,128)}, u32[]{:S(2)}) copy-start(s32[1,8,4096]{2,1,0:T(8,128)} %neighbours_hbm.1) | copy-start | bytes 393220
  6.5 0.9 %copy-start.5 = (f32[1,8,4096]{2,1,0:T(8,128)S(1)}, f32[1,8,4096]{2,1,0:T(8,128)}, u32[]{:S(2)}) copy-start(f32[1,8,4096]{2,1,0:T(8,128)} %coef_hbm.1) | copy-start | bytes 393220

commit v2 on v1

--- a/solution.py
+++ b/solution.py
@@ -19,6 +19,8 @@
 BLOCKS = CELLS // LANES
 CHUNKS = CAP // LANES
 ROWS = VARS * LEV
+SPAN = 2 * HALO // LANES + 1
+GU, SU, STU = 8, 8, 4
 FROM_LEFT, FROM_RIGHT = 0, HALO + CELLS
 
 
@@ -67,6 +69,8 @@
     table,
     sendbuf,
     recvbuf,
+    split,
+    forced,
     mixed,
     total,
     in_sems,
@@ -216,7 +220,7 @@
         to_peer(q).start()
         return c_
 
-    lax.fori_loop(0, PEERS, gather, 0)
+    lax.fori_loop(0, PEERS, gather, 0, unroll=GU)
 
     spread = (
         lax.rem(lax.broadcasted_iota(I32, (ROWS, LEV), 0), LEV)
@@ -233,43 +237,86 @@
         lax.broadcasted_iota(I32, (ROWS, ROWS), 1), LEV
     )
     mix_high, mix_low = halves(jnp.where(same, tiled, 0.0))
-    mix_high = jnp.concatenate([mix_high, mix_high], axis=1)
-    mix_low = jnp.concatenate([mix_low, mix_low], axis=1)
+    mix_both = jnp.concatenate(
+        [
+            jnp.concatenate([mix_high, mix_high], axis=1),
+            jnp.concatenate([mix_low, mix_low], axis=1),
+        ],
+        axis=0,
+    )
 
     loads[3].wait()
     loads[4].wait()
     for halo in halos:
         halo.wait_recv()
 
+    def split_block(e):
+        cells = pl.ds(pl.multiple_of(e * LANES, LANES), LANES)
+        for v in range(VARS):
+            at = pl.ds(pl.multiple_of(e * ROWS + v * LEV, LEV), LEV)
+            high, low = halves(ext[v, :, cells])
+            split[at, 0:LANES] = high
+            split[at, LANES : 2 * LANES] = low
+
+    for e in range(SPAN - 1):
+        split_block(e)
+
     def stencil(b, c_):
         base = pl.multiple_of(b * LANES, LANES)
+        split_block(b + SPAN - 1)
+        window = split[pl.ds(pl.multiple_of(b * ROWS, ROWS), SPAN * ROWS), :]
         near = nbr[:, pl.ds(base, LANES)]
         coefs = coef[:, pl.ds(base, LANES)]
-
-        def rows(r, s):
-            return ext[r // 2, (r % 2) * 8 : (r % 2) * 8 + 8, pl.ds(base + s * LANES, LANES)]
-
-        now = [rows(r, 2) for r in range(ROWS // 8)]
-        acc = list(now)
-        for j in range(NBR):
-            place = lane + near[j : j + 1]
-            at, block = place & (LANES - 1), place >> 7
-            factor = jnp.broadcast_to(coefs[j : j + 1], (8, LANES))
-            for r in range(ROWS // 8):
-                pick = lane_pick(rows(r, 0), at)
-                for s in range(1, 5):
-                    pick = jnp.where(block == s, lane_pick(rows(r, s), at), pick)
-                acc[r] = acc[r] + factor * (pick - now[r])
+        place = lane + near
+        at, block = (place & (LANES - 1)), place >> 7
+        rest = 1.0 - jnp.sum(coefs, axis=0, keepdims=True)
+        acc = [
+            rest * ext[r // 2, (r % 2) * 8 : (r % 2) * 8 + 8, pl.ds(HALO + base, LANES)]
+            for r in range(ROWS // 8)
+        ]
+        for pair in range(NBR // 2):
+            hot = jnp.concatenate(
+                [
+                    jnp.where(lane_rows == at[j : j + 1].astype(I16), one, nought)
+                    for j in (2 * pair, 2 * pair + 1)
+                ],
+                axis=1,
+            )
+            rows = jnp.dot(
+                window, jnp.concatenate([hot, hot], axis=0), preferred_element_type=F32
+            )
+            for half in range(2):
+                j = 2 * pair + half
+                factor = jnp.broadcast_to(coefs[j : j + 1], (8, LANES))
+                which = jnp.broadcast_to(block[j : j + 1], (8, LANES))
+                for r in range(ROWS // 8):
+                    pick = rows[r * 8 : r * 8 + 8, half * LANES : (half + 1) * LANES]
+                    for s in range(1, SPAN):
+                        pick = jnp.where(
+                            which == s,
+                            rows[
+                                s * ROWS + r * 8 : s * ROWS + r * 8 + 8,
+                                half * LANES : (half + 1) * LANES,
+                            ],
+                            pick,
+                        )
+                    acc[r] = acc[r] + factor * pick
         high, low = halves(jnp.concatenate(acc, axis=0))
-        both = jnp.concatenate([high, low], axis=0)
-        result = jnp.dot(mix_high, both, preferred_element_type=F32) + jnp.dot(
-            mix_low, both, preferred_element_type=F32
-        )
+        forced[0:ROWS, pl.ds(base, LANES)] = high
+        forced[ROWS : 2 * ROWS, pl.ds(base, LANES)] = low
+        return c_
+
+    lax.fori_loop(0, BLOCKS, stencil, 0, unroll=STU)
+
+    def mix(i, c_):
+        cells = pl.ds(pl.multiple_of(i * 4 * LANES, 4 * LANES), 4 * LANES)
+        result = jnp.dot(mix_both, forced[:, cells], preferred_element_type=F32)
+        result = result[0:ROWS] + result[ROWS : 2 * ROWS]
         for v in range(VARS):
-            mixed[v, :, pl.ds(base, LANES)] = result[v * LEV : (v + 1) * LEV]
+            mixed[v, :, cells] = result[v * LEV : (v + 1) * LEV]
         return c_
 
-    lax.fori_loop(0, BLOCKS, stencil, 0)
+    lax.fori_loop(0, BLOCKS // 4, mix, 0, unroll=2)
     store = pltpu.make_async_copy(mixed, mixed_hbm, out_sem)
     store.start()
 
@@ -301,7 +348,7 @@
         )
         return c_
 
-    lax.fori_loop(0, PEERS, scatter, 0)
+    lax.fori_loop(0, PEERS, scatter, 0, unroll=SU)
 
     for v in range(VARS):
         for b in range(BLOCKS):
@@ -354,6 +401,8 @@
             pltpu.VMEM((VARS * BLOCKS, LANES), F32),
             pltpu.VMEM((PEERS, VARS * CHUNKS, LANES), F32),
             pltpu.VMEM((PEERS, VARS * CHUNKS, LANES), F32),
+            pltpu.VMEM(((BLOCKS + SPAN - 1) * ROWS, 2 * LANES), BF16),
+            pltpu.VMEM((2 * ROWS, CELLS), BF16),
             pltpu.VMEM((VARS, LEV, CELLS), F32),
             pltpu.VMEM((2 * VARS * BLOCKS, LANES), F32),
             pltpu.SemaphoreType.DMA((6,)),
@@ -364,7 +413,7 @@
             pltpu.SemaphoreType.DMA,
         ],
         compiler_params=pltpu.CompilerParams(
-            collective_id=0, has_side_effects=True, vmem_limit_bytes=32 << 20
+            collective_id=0, has_side_effects=True, vmem_limit_bytes=60 << 20
         ),
         name="step",
     )(

time: 81.3 us -> 64.2 us (0.79)
  Pallas kernels: 71.8 us -> 59.5 us
  local copies, waits for them, and re-layouts: 7.38 us -> 1.44 us
  other arithmetic: 1.13 us -> 2.39 us
    pallas_call x1, Pallas kernels: 71.8 us -> 59.5 us  [local(): pl.pallas_call(kernel, out_shape=(jax.ShapeDtypeStruct((VARS, LEV, CELLS)...]
    unnamed x17 -> x3, local copies, waits for them, and re-layouts: 6.51 us -> 0.63 us
    broadcast_in_dim x1, other arithmetic: 1.13 us -> 2.39 us  [local(): return (updated[None], flux[None])]
where the time goes in v2:
time: 64.2 us; the launch traced here: 64 us
  Pallas kernels  59.5 us (93%)
  other arithmetic  2.39 us (4%)
  local copies, waits for them, and re-layouts  1.44 us (2%)
  between operations  0.65 us (1%)
    pallas_call x1, Pallas kernels, local(): pl.pallas_call(kernel, out_shape=(jax.ShapeDtypeStruct((VARS, LEV, CELLS)...  59.5 us
    broadcast_in_dim x1, other arithmetic, local(): return (updated[None], flux[None])  2.39 us

profile of v2, /device:TPU:1, one launch (start us, length us, event | category | flops | bytes accessed | tf_op | source)
XLA Modules:
  0.0 64.0 jit_solution(11584631234900306896)
XLA Ops:
  0.6 0.8 %slice_reduce_fusion = f32[16]{0:T(128)S(1)} fusion(f32[1,16,16]{2,1,0:T(8,128)} %mixing_ref.1), kind=kLoop, calls=%fused_computation.1 | loop fusion | bytes 128 | tf_op jit(solution)/shard_map/slice | solution.py:429
  1.4 59.5 %step.1 = (f32[4,16,4096]{2,1,0:T(8,128)}, f32[4,4096]{1,0:T(4,128)}) custom-call(f32[1,4,16,4096]{3,2,1,0:T(8,128)} %state_hbm.1, s32[1,8,4096]{2,1,0:T(8,128)} %neighbours_hbm.1, f32[1,8,4096]{2,1,0:T(8,128)} %coef_hbm.1, f32[1,16,16]{2,1,0:T(8,128)} %mixing_ref.1, s32[1,1,64]{2,1,0:T(1,128)} %count_ref.1, s32[1,1,64,1024]{3,2,1,0:T(8,128)} %source_hbm.1, ...), custom_call_target="tpu_custom_call" | custom-call | tf_op jit(solution)/shard_map/step/pallas_call | solution.py:383
  60.9 0.0 copy-start
  60.9 2.4 %add_bitcast_fusion = f32[1,4,16,4096]{3,2,1,0:T(8,128)} fusion(f32[4,16,4096]{2,1,0:T(8,128)} %get-tuple-element.4, f32[4,4096]{1,0:T(4,128)} %get-tuple-element.5, f32[16]{0:T(128)S(1)} %slice_reduce_fusion), kind=kLoop, calls=%fused_computation | loop fusion | flops 524288 | bytes 2162752 | tf_op jit(solution)/shard_map/broadcast_in_dim | solution.py:430
  63.3 0.0 copy-done
  63.3 0.6 copy.11
Async XLA Ops:
  60.9 2.4 %copy-start = (f32[4,4096]{1,0:T(4,128)S(1)}, f32[4,4096]{1,0:T(4,128)}, u32[]{:S(2)}) copy-start(f32[4,4096]{1,0:T(4,128)} %get-tuple-element.5) | copy-start | bytes 196612

commit v3 on v2

--- a/solution.py
+++ b/solution.py
@@ -1,4 +1,5 @@
-import functools
+import itertools
+import random
 
 import jax
 import jax.numpy as jnp
@@ -20,7 +21,8 @@
 CHUNKS = CAP // LANES
 ROWS = VARS * LEV
 SPAN = 2 * HALO // LANES + 1
-GU, SU, STU = 8, 8, 4
+BATCH = 16
+STENCIL_UNROLL = 4
 FROM_LEFT, FROM_RIGHT = 0, HALO + CELLS
 
 
@@ -37,11 +39,30 @@
     return jnp.take_along_axis(table, index, axis=0, mode="promise_in_bounds")
 
 
-def peer_at(me, step, sign):
+def displacements():
+    moves = list(itertools.product((0, 1, 2, -1), repeat=3))
+    random.Random(1).shuffle(moves)
+    ordered = []
+    for move in moves:
+        for one in (move, tuple(-m if m != 2 else 2 for m in move)):
+            if one not in ordered:
+                ordered.append(one)
+    ordered.sort(key=lambda move: -sum(abs(m) for m in move))
+    return [tuple(m % SIDE for m in move) for move in ordered]
+
+
+ORDER = displacements()
+
+
+def peer_at(me, group, k, sign):
     place = 0
-    for unit in (16, 4, 1):
+    for axis, unit in enumerate((16, 4, 1)):
         at = lax.rem(lax.div(me, unit), SIDE)
-        move = lax.rem(lax.div(step, unit), SIDE)
+        move = 0
+        for g in range(PEERS // BATCH):
+            step = ORDER[g * BATCH + k][axis]
+            if step:
+                move = move + jnp.where(group == g, step, 0)
         place = place + unit * lax.rem(at + sign * move + SIDE, SIDE)
     return place
 
@@ -176,8 +197,7 @@
             device_id_type=MESH,
         )
 
-    def gather(step, c_):
-        q = peer_at(me, step, 1)
+    def gather_one(q):
         cells = source[pl.ds(pl.multiple_of(q * CHUNKS, CHUNKS), CHUNKS), :]
         low, high = cells & (LANES - 1), cells >> 7
         used = jnp.where(
@@ -217,10 +237,16 @@
                     out[v] = jnp.where(sublane == c, pick, out[v])
         for v in range(VARS):
             sendbuf[q, v * 8 : v * 8 + 8, :] = out[v] * used
-        to_peer(q).start()
+
+    def gather(group, c_):
+        peers = [peer_at(me, group, k, 1) for k in range(BATCH)]
+        for q in peers:
+            gather_one(q)
+        for q in peers:
+            to_peer(q).start()
         return c_
 
-    lax.fori_loop(0, PEERS, gather, 0, unroll=GU)
+    lax.fori_loop(0, PEERS // BATCH, gather, 0)
 
     spread = (
         lax.rem(lax.broadcasted_iota(I32, (ROWS, LEV), 0), LEV)
@@ -306,7 +332,7 @@
         forced[ROWS : 2 * ROWS, pl.ds(base, LANES)] = low
         return c_
 
-    lax.fori_loop(0, BLOCKS, stencil, 0, unroll=STU)
+    lax.fori_loop(0, BLOCKS, stencil, 0, unroll=STENCIL_UNROLL)
 
     def mix(i, c_):
         cells = pl.ds(pl.multiple_of(i * 4 * LANES, 4 * LANES), 4 * LANES)
@@ -324,9 +350,7 @@
     by_peer(raw_target, target)
     total[...] = jnp.zeros_like(total)
 
-    def scatter(step, c_):
-        p = peer_at(me, step, -1)
-        from_peer(p).wait_recv()
+    def scatter_one(p):
         cells = target[pl.ds(pl.multiple_of(p * CHUNKS, CHUNKS), CHUNKS), :]
         low, high = (cells & (LANES - 1)), (cells >> 7)
         values, hots = [], []
@@ -346,9 +370,16 @@
             (((1,), (1,)), ((), ())),
             preferred_element_type=F32,
         )
+
+    def scatter(group, c_):
+        peers = [peer_at(me, group, k, -1) for k in range(BATCH)]
+        for p in peers:
+            from_peer(p).wait_recv()
+        for p in peers:
+            scatter_one(p)
         return c_
 
-    lax.fori_loop(0, PEERS, scatter, 0, unroll=SU)
+    lax.fori_loop(0, PEERS // BATCH, scatter, 0)
 
     for v in range(VARS):
         for b in range(BLOCKS):
@@ -365,6 +396,36 @@
     for halo in halos:
         halo.wait_send()
     store.wait()
+
+
+def finish(
+    mixed_hbm, flux_ref, mixing_ref, updated_hbm, flux_hbm, state, load_sems, store_sems, flux_sem
+):
+    loads = [
+        pltpu.make_async_copy(mixed_hbm.at[v], state.at[v], load_sems.at[v]) for v in range(VARS)
+    ]
+    for load in loads:
+        load.start()
+    flux_store = pltpu.make_async_copy(flux_ref, flux_hbm.at[0], flux_sem)
+    flux_store.start()
+    stores = []
+    shares = [
+        jnp.broadcast_to(mixing_ref[0, h * 8 : h * 8 + 8, 0:1], (8, LANES)) for h in range(LEV // 8)
+    ]
+    for v in range(VARS):
+        loads[v].wait()
+        for b in range(BLOCKS):
+            cells = slice(b * LANES, (b + 1) * LANES)
+            row = jnp.broadcast_to(flux_ref[v : v + 1, cells], (8, LANES))
+            for h in range(LEV // 8):
+                levels = slice(h * 8, h * 8 + 8)
+                state[v, levels, cells] = state[v, levels, cells] + shares[h] * row
+        store = pltpu.make_async_copy(state.at[v], updated_hbm.at[0, v], store_sems.at[v])
+        store.start()
+        stores.append(store)
+    for store in stores:
+        store.wait()
+    flux_store.wait()
 
 
 def local(
@@ -426,8 +487,23 @@
         remap_weight,
         remap_target,
     )
-    updated = mixed + column_mixing_operator[0, :, 0][None, :, None] * flux[:, None, :]
-    return updated[None], flux[None]
+    return pl.pallas_call(
+        finish,
+        out_shape=(
+            jax.ShapeDtypeStruct((1, VARS, LEV, CELLS), F32),
+            jax.ShapeDtypeStruct((1, VARS, CELLS), F32),
+        ),
+        in_specs=[hbm, vmem, vmem],
+        out_specs=(hbm, hbm),
+        scratch_shapes=[
+            pltpu.VMEM((VARS, LEV, CELLS), F32),
+            pltpu.SemaphoreType.DMA((VARS,)),
+            pltpu.SemaphoreType.DMA((VARS,)),
+            pltpu.SemaphoreType.DMA,
+        ],
+        compiler_params=pltpu.CompilerParams(vmem_limit_bytes=60 << 20),
+        name="finish",
+    )(mixed, flux, column_mixing_operator)
 
 
 def solution(mesh):

time: 64.2 us -> 41.7 us (0.65)
  Pallas kernels: 59.5 us -> 40.8 us
  other arithmetic: 2.39 us -> 0 us
  local copies, waits for them, and re-layouts: 1.44 us -> 0 us
    pallas_call x1, Pallas kernels: 59.5 us -> 38 us  [local(): pl.pallas_call(kernel, out_shape=(jax.ShapeDtypeStruct((VARS, LEV, CELLS)...]
    pallas_call x0 -> x1, Pallas kernels: none -> 2.88 us  [local(): pl.pallas_call(finish, out_shape=(jax.ShapeDtypeStruct((1, VARS, LEV, CEL...]
    broadcast_in_dim x1 -> x0, other arithmetic: 2.39 us -> none  [local(): return (updated[None], flux[None])]
    slice x1 -> x0, local copies, waits for them, and re-layouts: 0.81 us -> none  [local(): column_mixing_operator[0, :, 0][None, :, None] * flux[:, None, :]]
where the time goes in v3:
time: 41.7 us; the launch traced here: 41.5 us
  Pallas kernels  40.8 us (98%)
  between operations  0.64 us (2%)
    pallas_call x1, Pallas kernels, local(): pl.pallas_call(kernel, out_shape=(jax.ShapeDtypeStruct((VARS, LEV, CELLS)...  38 us
    pallas_call x1, Pallas kernels, local(): pl.pallas_call(finish, out_shape=(jax.ShapeDtypeStruct((1, VARS, LEV, CEL...  2.88 us

profile of v3, /device:TPU:1, one launch (start us, length us, event | category | flops | bytes accessed | tf_op | source)
XLA Modules:
  0.0 41.5 jit_solution(3073601179188160329)
XLA Ops:
  0.6 38.0 %step.1 = (f32[4,16,4096]{2,1,0:T(8,128)}, f32[4,4096]{1,0:T(4,128)}) custom-call(f32[1,4,16,4096]{3,2,1,0:T(8,128)} %state_hbm.1, s32[1,8,4096]{2,1,0:T(8,128)} %neighbours_hbm.1, f32[1,8,4096]{2,1,0:T(8,128)} %coef_hbm.1, f32[1,16,16]{2,1,0:T(8,128)} %mixing_ref.3, s32[1,1,64]{2,1,0:T(1,128)} %count_ref.1, s32[1,1,64,1024]{3,2,1,0:T(8,128)} %source_hbm.1, ...), custom_call_target="tpu_custom_call" | custom-call | tf_op jit(solution)/shard_map/step/pallas_call | solution.py:444
  38.6 2.9 %finish.1 = (f32[1,4,16,4096]{3,2,1,0:T(8,128)}, f32[1,4,4096]{2,1,0:T(4,128)}) custom-call(f32[4,16,4096]{2,1,0:T(8,128)} %get-tuple-element.4.mixed_hbm, f32[4,4096]{1,0:T(4,128)} %get-tuple-element.5.flux_ref, f32[1,16,16]{2,1,0:T(8,128)} %mixing_ref.3), custom_call_target="tpu_custom_call" | custom-call | tf_op jit(solution)/shard_map/finish/pallas_call | solution.py:490

commit v4 on v3

--- a/solution.py
+++ b/solution.py
@@ -23,6 +23,7 @@
 SPAN = 2 * HALO // LANES + 1
 BATCH = 16
 STENCIL_UNROLL = 4
+PRODUCTS = 4
 FROM_LEFT, FROM_RIGHT = 0, HALO + CELLS
 
 
@@ -71,14 +72,18 @@
     state_hbm,
     neighbours_hbm,
     coef_hbm,
-    mixing_ref,
-    count_ref,
+    mixing_hbm,
+    count_hbm,
     source_hbm,
     weight_hbm,
     target_hbm,
     mixed_hbm,
-    flux_ref,
+    flux_hbm,
     ext,
+    blended,
+    mixing,
+    count,
+    flux,
     nbr,
     coef,
     raw_source,
@@ -91,7 +96,6 @@
     sendbuf,
     recvbuf,
     split,
-    forced,
     mixed,
     total,
     in_sems,
@@ -99,27 +103,31 @@
     halo_recv_sems,
     send_sems,
     recv_sems,
-    out_sem,
+    out_sems,
+    flux_sem,
 ):
     comp, me = lax.axis_index("comp"), lax.axis_index("dom")
     other = 1 - comp
     right, left = lax.rem(me + 1, PEERS), lax.rem(me + PEERS - 1, PEERS)
 
-    loads = [
-        pltpu.make_async_copy(src, dst, in_sems.at[i])
-        for i, (src, dst) in enumerate(
-            (
-                (state_hbm.at[0], ext.at[:, :, pl.ds(HALO, CELLS)]),
-                (source_hbm.at[0, 0], raw_source),
-                (weight_hbm.at[0, 0], raw_weight),
-                (neighbours_hbm.at[0], nbr),
-                (coef_hbm.at[0], coef),
-                (target_hbm.at[0, 0], raw_target),
-            )
-        )
+    def load(i, src, dst):
+        return pltpu.make_async_copy(src, dst, in_sems.at[i])
+
+    inner = pl.ds(HALO, CELLS)
+    state_loads = [
+        load(h, state_hbm.at[0, :, pl.ds(8 * h, 8), :], ext.at[:, pl.ds(8 * h, 8), inner])
+        for h in range(2)
     ]
-    for load in loads:
-        load.start()
+    source_load = load(2, source_hbm.at[0, 0], raw_source)
+    weight_load = load(3, weight_hbm.at[0, 0], raw_weight)
+    count_load = load(4, count_hbm.at[0], count)
+    early = [state_loads[0], source_load, weight_load, count_load]
+    mixing_load = load(5, mixing_hbm.at[0], mixing)
+    target_load = load(6, target_hbm.at[0, 0], raw_target)
+    stencil_loads = [load(7, neighbours_hbm.at[0], nbr), load(8, coef_hbm.at[0], coef)]
+    late = [state_loads[1], mixing_load, *stencil_loads, target_load]
+    for one_load in early + late:
+        one_load.start()
 
     barrier = pltpu.get_barrier_semaphore()
 
@@ -131,7 +139,7 @@
     for side in (left, right):
         pl.semaphore_signal(barrier, inc=1, device_id=(comp, side), device_id_type=MESH)
 
-    loads[0].wait()
+    state_loads[0].wait()
     for v in range(VARS):
         for b in range(BLOCKS):
             table[v * BLOCKS + b : v * BLOCKS + b + 1, :] = ext[
@@ -139,8 +147,9 @@
             ]
     table_halves = jnp.concatenate(halves(table[...]), axis=1)
 
-    loads[1].wait()
-    loads[2].wait()
+    source_load.wait()
+    weight_load.wait()
+    count_load.wait()
 
     def by_peer(raw, tidy):
         for g in range(PEERS // 8):
@@ -151,8 +160,6 @@
 
     by_peer(raw_source, source)
     by_peer(raw_weight, weight)
-
-    pl.semaphore_wait(barrier, PEERS + 2)
 
     halos = [
         pltpu.make_async_remote_copy(
@@ -167,8 +174,6 @@
             ((CELLS - HALO, FROM_LEFT, right), (0, FROM_RIGHT, left))
         )
     ]
-    for halo in halos:
-        halo.start()
 
     sublane = lax.broadcasted_iota(I32, (8, LANES), 0)
     lane = lax.broadcasted_iota(I32, (8, LANES), 1)
@@ -201,7 +206,7 @@
         cells = source[pl.ds(pl.multiple_of(q * CHUNKS, CHUNKS), CHUNKS), :]
         low, high = cells & (LANES - 1), cells >> 7
         used = jnp.where(
-            slot < count_ref[0, 0, q],
+            slot < count[0, q],
             weight[pl.ds(pl.multiple_of(q * CHUNKS, CHUNKS), CHUNKS), :],
             0.0,
         )
@@ -242,18 +247,26 @@
         peers = [peer_at(me, group, k, 1) for k in range(BATCH)]
         for q in peers:
             gather_one(q)
+
+        @pl.when(group == 0)
+        def _():
+            pl.semaphore_wait(barrier, PEERS + 2)
+            for halo in halos:
+                halo.start()
+
         for q in peers:
             to_peer(q).start()
         return c_
 
     lax.fori_loop(0, PEERS // BATCH, gather, 0)
 
+    mixing_load.wait()
     spread = (
         lax.rem(lax.broadcasted_iota(I32, (ROWS, LEV), 0), LEV)
         == lax.broadcasted_iota(I32, (ROWS, LEV), 1)
     ).astype(F32)
     tiled = lax.dot_general(
-        jnp.dot(spread, mixing_ref[0], precision=lax.Precision.HIGHEST, preferred_element_type=F32),
+        jnp.dot(spread, mixing[...], precision=lax.Precision.HIGHEST, preferred_element_type=F32),
         spread,
         (((1,), (1,)), ((), ())),
         precision=lax.Precision.HIGHEST,
@@ -271,36 +284,42 @@
         axis=0,
     )
 
-    loads[3].wait()
-    loads[4].wait()
+    state_loads[1].wait()
     for halo in halos:
         halo.wait_recv()
 
-    def split_block(e):
-        cells = pl.ds(pl.multiple_of(e * LANES, LANES), LANES)
+    def blend(i, c_):
+        cells = pl.ds(pl.multiple_of(i * 4 * LANES, 4 * LANES), 4 * LANES)
+        both = jnp.concatenate(
+            [halves(ext[v, :, cells])[part] for part in range(2) for v in range(VARS)], axis=0
+        )
+        result = jnp.dot(mix_both, both, preferred_element_type=F32)
+        result = result[0:ROWS] + result[ROWS : 2 * ROWS]
         for v in range(VARS):
-            at = pl.ds(pl.multiple_of(e * ROWS + v * LEV, LEV), LEV)
-            high, low = halves(ext[v, :, cells])
-            split[at, 0:LANES] = high
-            split[at, LANES : 2 * LANES] = low
-
-    for e in range(SPAN - 1):
-        split_block(e)
+            blended[v, :, cells] = result[v * LEV : (v + 1) * LEV]
+        high, low = halves(result)
+        for e in range(4):
+            at = pl.ds(pl.multiple_of((i * 4 + e) * ROWS, ROWS), ROWS)
+            split[at, 0:LANES] = high[:, e * LANES : (e + 1) * LANES]
+            split[at, LANES : 2 * LANES] = low[:, e * LANES : (e + 1) * LANES]
+        return c_
+
+    lax.fori_loop(0, (BLOCKS + SPAN - 1) // 4, blend, 0, unroll=3)
+    for one_load in stencil_loads:
+        one_load.wait()
+
+    def rows_at(r, cells):
+        return blended[r // 2, (r % 2) * 8 : (r % 2) * 8 + 8, cells]
 
     def stencil(b, c_):
         base = pl.multiple_of(b * LANES, LANES)
-        split_block(b + SPAN - 1)
         window = split[pl.ds(pl.multiple_of(b * ROWS, ROWS), SPAN * ROWS), :]
-        near = nbr[:, pl.ds(base, LANES)]
         coefs = coef[:, pl.ds(base, LANES)]
-        place = lane + near
+        place = lane + nbr[:, pl.ds(base, LANES)]
         at, block = (place & (LANES - 1)), place >> 7
         rest = 1.0 - jnp.sum(coefs, axis=0, keepdims=True)
-        acc = [
-            rest * ext[r // 2, (r % 2) * 8 : (r % 2) * 8 + 8, pl.ds(HALO + base, LANES)]
-            for r in range(ROWS // 8)
-        ]
-        for pair in range(NBR // 2):
+        acc = [rest * rows_at(r, pl.ds(HALO + base, LANES)) for r in range(ROWS // 8)]
+        for pair in range(PRODUCTS // 2):
             hot = jnp.concatenate(
                 [
                     jnp.where(lane_rows == at[j : j + 1].astype(I16), one, nought)
@@ -315,38 +334,40 @@
                 j = 2 * pair + half
                 factor = jnp.broadcast_to(coefs[j : j + 1], (8, LANES))
                 which = jnp.broadcast_to(block[j : j + 1], (8, LANES))
+                lanes = slice(half * LANES, (half + 1) * LANES)
                 for r in range(ROWS // 8):
-                    pick = rows[r * 8 : r * 8 + 8, half * LANES : (half + 1) * LANES]
+                    pick = rows[r * 8 : r * 8 + 8, lanes]
                     for s in range(1, SPAN):
-                        pick = jnp.where(
-                            which == s,
-                            rows[
-                                s * ROWS + r * 8 : s * ROWS + r * 8 + 8,
-                                half * LANES : (half + 1) * LANES,
-                            ],
-                            pick,
-                        )
+                        row = s * ROWS + r * 8
+                        pick = jnp.where(which == s, rows[row : row + 8, lanes], pick)
                     acc[r] = acc[r] + factor * pick
-        high, low = halves(jnp.concatenate(acc, axis=0))
-        forced[0:ROWS, pl.ds(base, LANES)] = high
-        forced[ROWS : 2 * ROWS, pl.ds(base, LANES)] = low
+        for r in range(ROWS // 8):
+            mixed[r // 2, (r % 2) * 8 : (r % 2) * 8 + 8, pl.ds(base, LANES)] = acc[r]
         return c_
 
     lax.fori_loop(0, BLOCKS, stencil, 0, unroll=STENCIL_UNROLL)
 
-    def mix(i, c_):
-        cells = pl.ds(pl.multiple_of(i * 4 * LANES, 4 * LANES), 4 * LANES)
-        result = jnp.dot(mix_both, forced[:, cells], preferred_element_type=F32)
-        result = result[0:ROWS] + result[ROWS : 2 * ROWS]
-        for v in range(VARS):
-            mixed[v, :, cells] = result[v * LEV : (v + 1) * LEV]
-        return c_
-
-    lax.fori_loop(0, BLOCKS // 4, mix, 0, unroll=2)
-    store = pltpu.make_async_copy(mixed, mixed_hbm, out_sem)
-    store.start()
-
-    loads[5].wait()
+    def permuted(b, rows):
+        base = pl.multiple_of(b * LANES, LANES)
+        cells = pl.ds(base, LANES)
+        coefs = coef[:, cells]
+        place = lane + nbr[:, cells]
+        at, block = (place & (LANES - 1)), place >> 7
+        acc = [mixed[r // 2, (r % 2) * 8 : (r % 2) * 8 + 8, cells] for r in rows]
+        for j in range(PRODUCTS, NBR):
+            turn = jnp.broadcast_to(at[j : j + 1], (8, LANES))
+            which = jnp.broadcast_to(block[j : j + 1], (8, LANES))
+            factor = jnp.broadcast_to(coefs[j : j + 1], (8, LANES))
+            for i, r in enumerate(rows):
+                pick = lane_pick(rows_at(r, cells), turn)
+                for s in range(1, SPAN):
+                    other_pick = lane_pick(rows_at(r, pl.ds(base + s * LANES, LANES)), turn)
+                    pick = jnp.where(which == s, other_pick, pick)
+                acc[i] = acc[i] + factor * pick
+        for i, r in enumerate(rows):
+            mixed[r // 2, (r % 2) * 8 : (r % 2) * 8 + 8, cells] = acc[i]
+
+    target_load.wait()
     by_peer(raw_target, target)
     total[...] = jnp.zeros_like(total)
 
@@ -371,12 +392,22 @@
             preferred_element_type=F32,
         )
 
+    def store_of(group):
+        width = CELLS * BATCH // PEERS
+        cells = pl.ds(pl.multiple_of(group * width, width), width)
+        return pltpu.make_async_copy(
+            mixed.at[:, :, cells], mixed_hbm.at[:, :, cells], out_sems.at[group]
+        )
+
     def scatter(group, c_):
         peers = [peer_at(me, group, k, -1) for k in range(BATCH)]
         for p in peers:
             from_peer(p).wait_recv()
-        for p in peers:
+        for k, p in enumerate(peers):
             scatter_one(p)
+            half = ROWS // 16
+            permuted(group * (BATCH // 2) + k // 2, range(k % 2 * half, (k % 2 + 1) * half))
+        store_of(group).start()
         return c_
 
     lax.fori_loop(0, PEERS // BATCH, scatter, 0)
@@ -384,9 +415,12 @@
     for v in range(VARS):
         for b in range(BLOCKS):
             r = v * BLOCKS + b
-            flux_ref[v : v + 1, b * LANES : (b + 1) * LANES] = (
+            flux[v : v + 1, b * LANES : (b + 1) * LANES] = (
                 total[r : r + 1, :] + total[r + VARS * BLOCKS : r + VARS * BLOCKS + 1, :]
             )
+
+    flux_store = pltpu.make_async_copy(flux, flux_hbm, flux_sem)
+    flux_store.start()
 
     def sent(step, c_):
         to_peer(step).wait_send()
@@ -395,28 +429,34 @@
     lax.fori_loop(0, PEERS, sent, 0)
     for halo in halos:
         halo.wait_send()
-    store.wait()
+    for group in range(PEERS // BATCH):
+        store_of(group).wait()
+    flux_store.wait()
 
 
 def finish(
-    mixed_hbm, flux_ref, mixing_ref, updated_hbm, flux_hbm, state, load_sems, store_sems, flux_sem
+    mixed_hbm, flux_in, mixing_hbm, updated_hbm, flux_out, state, flux, mixing, load_sems, store_sems
 ):
     loads = [
         pltpu.make_async_copy(mixed_hbm.at[v], state.at[v], load_sems.at[v]) for v in range(VARS)
     ]
-    for load in loads:
+    flux_load = pltpu.make_async_copy(flux_in, flux, load_sems.at[VARS])
+    mixing_load = pltpu.make_async_copy(mixing_hbm.at[0], mixing, load_sems.at[VARS + 1])
+    for load in [flux_load, mixing_load, *loads]:
         load.start()
-    flux_store = pltpu.make_async_copy(flux_ref, flux_hbm.at[0], flux_sem)
+    flux_load.wait()
+    mixing_load.wait()
+    flux_store = pltpu.make_async_copy(flux, flux_out.at[0], store_sems.at[VARS])
     flux_store.start()
     stores = []
     shares = [
-        jnp.broadcast_to(mixing_ref[0, h * 8 : h * 8 + 8, 0:1], (8, LANES)) for h in range(LEV // 8)
+        jnp.broadcast_to(mixing[h * 8 : h * 8 + 8, 0:1], (8, LANES)) for h in range(LEV // 8)
     ]
     for v in range(VARS):
         loads[v].wait()
         for b in range(BLOCKS):
             cells = slice(b * LANES, (b + 1) * LANES)
-            row = jnp.broadcast_to(flux_ref[v : v + 1, cells], (8, LANES))
+            row = jnp.broadcast_to(flux[v : v + 1, cells], (8, LANES))
             for h in range(LEV // 8):
                 levels = slice(h * 8, h * 8 + 8)
                 state[v, levels, cells] = state[v, levels, cells] + shares[h] * row
@@ -439,18 +479,20 @@
     remap_target,
 ):
     hbm = pl.BlockSpec(memory_space=pltpu.HBM)
-    vmem = pl.BlockSpec(memory_space=pltpu.VMEM)
-    smem = pl.BlockSpec(memory_space=pltpu.SMEM)
     mixed, flux = pl.pallas_call(
         kernel,
         out_shape=(
             jax.ShapeDtypeStruct((VARS, LEV, CELLS), F32),
             jax.ShapeDtypeStruct((VARS, CELLS), F32),
         ),
-        in_specs=[hbm, hbm, hbm, vmem, smem, hbm, hbm, hbm],
-        out_specs=(hbm, vmem),
+        in_specs=[hbm] * 8,
+        out_specs=(hbm, hbm),
         scratch_shapes=[
             pltpu.VMEM((VARS, LEV, CELLS + 2 * HALO), F32),
+            pltpu.VMEM((VARS, LEV, CELLS + 2 * HALO), F32),
+            pltpu.VMEM((LEV, LEV), F32),
+            pltpu.SMEM((1, PEERS), I32),
+            pltpu.VMEM((VARS, CELLS), F32),
             pltpu.VMEM((NBR, CELLS), I32),
             pltpu.VMEM((NBR, CELLS), F32),
             pltpu.VMEM((PEERS, CAP), I32),
@@ -463,14 +505,14 @@
             pltpu.VMEM((PEERS, VARS * CHUNKS, LANES), F32),
             pltpu.VMEM((PEERS, VARS * CHUNKS, LANES), F32),
             pltpu.VMEM(((BLOCKS + SPAN - 1) * ROWS, 2 * LANES), BF16),
-            pltpu.VMEM((2 * ROWS, CELLS), BF16),
             pltpu.VMEM((VARS, LEV, CELLS), F32),
             pltpu.VMEM((2 * VARS * BLOCKS, LANES), F32),
-            pltpu.SemaphoreType.DMA((6,)),
+            pltpu.SemaphoreType.DMA((9,)),
             pltpu.SemaphoreType.DMA((2,)),
             pltpu.SemaphoreType.DMA((2,)),
             pltpu.SemaphoreType.DMA((PEERS,)),
             pltpu.SemaphoreType.DMA((PEERS,)),
+            pltpu.SemaphoreType.DMA((PEERS // BATCH,)),
             pltpu.SemaphoreType.DMA,
         ],
         compiler_params=pltpu.CompilerParams(
@@ -493,13 +535,14 @@
             jax.ShapeDtypeStruct((1, VARS, LEV, CELLS), F32),
             jax.ShapeDtypeStruct((1, VARS, CELLS), F32),
         ),
-        in_specs=[hbm, vmem, vmem],
+        in_specs=[hbm] * 3,
         out_specs=(hbm, hbm),
         scratch_shapes=[
             pltpu.VMEM((VARS, LEV, CELLS), F32),
-            pltpu.SemaphoreType.DMA((VARS,)),
-            pltpu.SemaphoreType.DMA((VARS,)),
-            pltpu.SemaphoreType.DMA,
+            pltpu.VMEM((VARS, CELLS), F32),
+            pltpu.VMEM((LEV, LEV), F32),
+            pltpu.SemaphoreType.DMA((VARS + 2,)),
+            pltpu.SemaphoreType.DMA((VARS + 1,)),
         ],
         compiler_params=pltpu.CompilerParams(vmem_limit_bytes=60 << 20),
         name="finish",

time: 41.7 us -> 40.5 us (0.971)
  the two profiles are of different devices: /device:TPU:1 before, /device:TPU:58 now
where the time goes in v4:
time: 40.5 us; the launch traced here: 40.4 us
  Pallas kernels  39.7 us (98%)
  between operations  0.64 us (2%)
    pallas_call x1, Pallas kernels, local(): pl.pallas_call(kernel, out_shape=(jax.ShapeDtypeStruct((VARS, LEV, CELLS)...  37.7 us
    pallas_call x1, Pallas kernels, local(): pl.pallas_call(finish, out_shape=(jax.ShapeDtypeStruct((1, VARS, LEV, CEL...  2.09 us

profile of v4, /device:TPU:58, one launch (start us, length us, event | category | flops | bytes accessed | tf_op | source)
XLA Modules:
  0.0 40.4 jit_solution(1330316486063228466)
XLA Ops:
  0.6 37.7 %step.1 = (f32[4,16,4096]{2,1,0:T(8,128)}, f32[4,4096]{1,0:T(4,128)}) custom-call(f32[1,4,16,4096]{3,2,1,0:T(8,128)} %state_hbm.1, s32[1,8,4096]{2,1,0:T(8,128)} %neighbours_hbm.1, f32[1,8,4096]{2,1,0:T(8,128)} %coef_hbm.1, f32[1,16,16]{2,1,0:T(8,128)} %mixing_hbm.3, s32[1,1,64]{2,1,0:T(1,128)} %count_hbm.1, s32[1,1,64,1024]{3,2,1,0:T(8,128)} %source_hbm.1, ...), custom_call_target="tpu_custom_call" | custom-call | tf_op jit(solution)/shard_map/step/pallas_call | solution.py:482
  38.3 2.1 %finish.1 = (f32[1,4,16,4096]{3,2,1,0:T(8,128)}, f32[1,4,4096]{2,1,0:T(4,128)}) custom-call(f32[4,16,4096]{2,1,0:T(8,128)} %get-tuple-element.4.mixed_hbm, f32[4,4096]{1,0:T(4,128)} %get-tuple-element.5.flux_in, f32[1,16,16]{2,1,0:T(8,128)} %mixing_hbm.3), custom_call_target="tpu_custom_call" | custom-call | tf_op jit(solution)/shard_map/finish/pallas_call | solution.py:532

commit v5 on v4

--- a/solution.py
+++ b/solution.py
@@ -48,23 +48,28 @@
         for one in (move, tuple(-m if m != 2 else 2 for m in move)):
             if one not in ordered:
                 ordered.append(one)
-    ordered.sort(key=lambda move: -sum(abs(m) for m in move))
+    ordered.sort(key=lambda move: sum(abs(m) for m in move))
     return [tuple(m % SIDE for m in move) for move in ordered]
 
 
 ORDER = displacements()
 
 
-def peer_at(me, group, k, sign):
+def places(me, sign):
+    return [
+        [
+            unit * lax.rem(lax.rem(lax.div(me, unit), SIDE) + sign * move + SIDE, SIDE)
+            for move in range(SIDE)
+        ]
+        for unit in (SIDE * SIDE, SIDE, 1)
+    ]
+
+
+def peer_at(places_, group, k):
     place = 0
-    for axis, unit in enumerate((16, 4, 1)):
-        at = lax.rem(lax.div(me, unit), SIDE)
-        move = 0
-        for g in range(PEERS // BATCH):
-            step = ORDER[g * BATCH + k][axis]
-            if step:
-                move = move + jnp.where(group == g, step, 0)
-        place = place + unit * lax.rem(at + sign * move + SIDE, SIDE)
+    for g in range(PEERS // BATCH):
+        there = sum(places_[axis][move] for axis, move in enumerate(ORDER[g * BATCH + k]))
+        place = there if g == 0 else jnp.where(group == g, there, place)
     return place
 
 
@@ -101,7 +106,7 @@
     in_sems,
     halo_send_sems,
     halo_recv_sems,
-    send_sems,
+    send_sem,
     recv_sems,
     out_sems,
     flux_sem,
@@ -182,23 +187,25 @@
     block_rows = lax.broadcasted_iota(I32, (BLOCKS, 1), 0).astype(I16)
     one, nought = BF16(1), BF16(0)
 
-    def to_peer(q):
+    ahead, behind = places(me, 1), places(me, -1)
+
+    def to_peer(q, group):
         return pltpu.make_async_remote_copy(
             src_ref=sendbuf.at[q],
             dst_ref=recvbuf.at[me],
-            send_sem=send_sems.at[q],
-            recv_sem=recv_sems.at[me],
+            send_sem=send_sem,
+            recv_sem=recv_sems.at[group],
             device_id=(other, q),
             device_id_type=MESH,
         )
 
-    def from_peer(p):
+    def many(count, group):
         return pltpu.make_async_remote_copy(
-            src_ref=sendbuf.at[p],
-            dst_ref=recvbuf.at[p],
-            send_sem=send_sems.at[p],
-            recv_sem=recv_sems.at[p],
-            device_id=(other, p),
+            src_ref=sendbuf.at[pl.ds(0, count)],
+            dst_ref=recvbuf.at[pl.ds(0, count)],
+            send_sem=send_sem,
+            recv_sem=recv_sems.at[group],
+            device_id=(other, me),
             device_id_type=MESH,
         )
 
@@ -244,7 +251,7 @@
             sendbuf[q, v * 8 : v * 8 + 8, :] = out[v] * used
 
     def gather(group, c_):
-        peers = [peer_at(me, group, k, 1) for k in range(BATCH)]
+        peers = [peer_at(ahead, group, k) for k in range(BATCH)]
         for q in peers:
             gather_one(q)
 
@@ -255,7 +262,7 @@
                 halo.start()
 
         for q in peers:
-            to_peer(q).start()
+            to_peer(q, group).start()
         return c_
 
     lax.fori_loop(0, PEERS // BATCH, gather, 0)
@@ -400,9 +407,8 @@
         )
 
     def scatter(group, c_):
-        peers = [peer_at(me, group, k, -1) for k in range(BATCH)]
-        for p in peers:
-            from_peer(p).wait_recv()
+        peers = [peer_at(behind, group, k) for k in range(BATCH)]
+        many(BATCH, group).wait_recv()
         for k, p in enumerate(peers):
             scatter_one(p)
             half = ROWS // 16
@@ -422,11 +428,7 @@
     flux_store = pltpu.make_async_copy(flux, flux_hbm, flux_sem)
     flux_store.start()
 
-    def sent(step, c_):
-        to_peer(step).wait_send()
-        return c_
-
-    lax.fori_loop(0, PEERS, sent, 0)
+    many(PEERS, 0).wait_send()
     for halo in halos:
         halo.wait_send()
     for group in range(PEERS // BATCH):
@@ -510,8 +512,8 @@
             pltpu.SemaphoreType.DMA((9,)),
             pltpu.SemaphoreType.DMA((2,)),
             pltpu.SemaphoreType.DMA((2,)),
-            pltpu.SemaphoreType.DMA((PEERS,)),
-            pltpu.SemaphoreType.DMA((PEERS,)),
+            pltpu.SemaphoreType.DMA,
+            pltpu.SemaphoreType.DMA((PEERS // BATCH,)),
             pltpu.SemaphoreType.DMA((PEERS // BATCH,)),
             pltpu.SemaphoreType.DMA,
         ],

time: 40.5 us -> 36.1 us (0.89)
  the two profiles are of different devices: /device:TPU:58 before, /device:TPU:3 now
where the time goes in v5:
time: 36.1 us; the launch traced here: 36 us
  Pallas kernels  35.4 us (98%)
  between operations  0.64 us (2%)
    pallas_call x1, Pallas kernels, local(): pl.pallas_call(kernel, out_shape=(jax.ShapeDtypeStruct((VARS, LEV, CELLS)...  33.3 us
    pallas_call x1, Pallas kernels, local(): pl.pallas_call(finish, out_shape=(jax.ShapeDtypeStruct((1, VARS, LEV, CEL...  2.09 us

profile of v5, /device:TPU:3, one launch (start us, length us, event | category | flops | bytes accessed | tf_op | source)
XLA Modules:
  0.0 36.0 jit_solution(10851289523351034040)
XLA Ops:
  0.6 33.3 %step.1 = (f32[4,16,4096]{2,1,0:T(8,128)}, f32[4,4096]{1,0:T(4,128)}) custom-call(f32[1,4,16,4096]{3,2,1,0:T(8,128)} %state_hbm.1, s32[1,8,4096]{2,1,0:T(8,128)} %neighbours_hbm.1, f32[1,8,4096]{2,1,0:T(8,128)} %coef_hbm.1, f32[1,16,16]{2,1,0:T(8,128)} %mixing_hbm.3, s32[1,1,64]{2,1,0:T(1,128)} %count_hbm.1, s32[1,1,64,1024]{3,2,1,0:T(8,128)} %source_hbm.1, ...), custom_call_target="tpu_custom_call" | custom-call | tf_op jit(solution)/shard_map/step/pallas_call | solution.py:484
  33.9 2.1 %finish.1 = (f32[1,4,16,4096]{3,2,1,0:T(8,128)}, f32[1,4,4096]{2,1,0:T(4,128)}) custom-call(f32[4,16,4096]{2,1,0:T(8,128)} %get-tuple-element.4.mixed_hbm, f32[4,4096]{1,0:T(4,128)} %get-tuple-element.5.flux_in, f32[1,16,16]{2,1,0:T(8,128)} %mixing_hbm.3), custom_call_target="tpu_custom_call" | custom-call | tf_op jit(solution)/shard_map/finish/pallas_call | solution.py:534

commit v6 on v5

--- a/solution.py
+++ b/solution.py
@@ -22,6 +22,7 @@
 ROWS = VARS * LEV
 SPAN = 2 * HALO // LANES + 1
 BATCH = 16
+SENT = 8
 STENCIL_UNROLL = 4
 PRODUCTS = 4
 FROM_LEFT, FROM_RIGHT = 0, HALO + CELLS
@@ -65,10 +66,10 @@
     ]
 
 
-def peer_at(places_, group, k):
+def peer_at(places_, group, batch, k):
     place = 0
-    for g in range(PEERS // BATCH):
-        there = sum(places_[axis][move] for axis, move in enumerate(ORDER[g * BATCH + k]))
+    for g in range(PEERS // batch):
+        there = sum(places_[axis][move] for axis, move in enumerate(ORDER[g * batch + k]))
         place = there if g == 0 else jnp.where(group == g, there, place)
     return place
 
@@ -251,7 +252,7 @@
             sendbuf[q, v * 8 : v * 8 + 8, :] = out[v] * used
 
     def gather(group, c_):
-        peers = [peer_at(ahead, group, k) for k in range(BATCH)]
+        peers = [peer_at(ahead, group, SENT, k) for k in range(SENT)]
         for q in peers:
             gather_one(q)
 
@@ -262,10 +263,10 @@
                 halo.start()
 
         for q in peers:
-            to_peer(q, group).start()
+            to_peer(q, lax.div(group, BATCH // SENT) + jnp.where(group == PEERS // SENT - 1, 1, 0)).start()
         return c_
 
-    lax.fori_loop(0, PEERS // BATCH, gather, 0)
+    lax.fori_loop(0, PEERS // SENT, gather, 0)
 
     mixing_load.wait()
     spread = (
@@ -406,17 +407,29 @@
             mixed.at[:, :, cells], mixed_hbm.at[:, :, cells], out_sems.at[group]
         )
 
-    def scatter(group, c_):
-        peers = [peer_at(behind, group, k) for k in range(BATCH)]
-        many(BATCH, group).wait_recv()
+    def arrived(group, batch, sem):
+        peers = [peer_at(behind, group, batch, k) for k in range(batch)]
+        many(batch, sem).wait_recv()
+        half = ROWS // 16
         for k, p in enumerate(peers):
             scatter_one(p)
-            half = ROWS // 16
-            permuted(group * (BATCH // 2) + k // 2, range(k % 2 * half, (k % 2 + 1) * half))
+            permuted(group * (batch // 2) + k // 2, range(k % 2 * half, (k % 2 + 1) * half))
+
+    last = PEERS // BATCH - 1
+
+    def scatter(group, c_):
+        arrived(group, BATCH, group)
         store_of(group).start()
         return c_
 
-    lax.fori_loop(0, PEERS // BATCH, scatter, 0)
+    lax.fori_loop(0, last, scatter, 0)
+
+    def scatter_last(part, c_):
+        arrived(part + last * (BATCH // SENT), SENT, part + last)
+        return c_
+
+    lax.fori_loop(0, BATCH // SENT, scatter_last, 0)
+    store_of(last).start()
 
     for v in range(VARS):
         for b in range(BLOCKS):
@@ -513,7 +526,7 @@
             pltpu.SemaphoreType.DMA((2,)),
             pltpu.SemaphoreType.DMA((2,)),
             pltpu.SemaphoreType.DMA,
-            pltpu.SemaphoreType.DMA((PEERS // BATCH,)),
+            pltpu.SemaphoreType.DMA((PEERS // BATCH + 1,)),
             pltpu.SemaphoreType.DMA((PEERS // BATCH,)),
             pltpu.SemaphoreType.DMA,
         ],

time: 36.1 us -> 35.5 us (0.983)
  the two profiles are of different devices: /device:TPU:3 before, /device:TPU:1 now
where the time goes in v6:
time: 35.5 us; the launch traced here: 35.4 us
  Pallas kernels  34.7 us (98%)
  between operations  0.64 us (2%)
    pallas_call x1, Pallas kernels, local(): pl.pallas_call(kernel, out_shape=(jax.ShapeDtypeStruct((VARS, LEV, CELLS)...  32.6 us
    pallas_call x1, Pallas kernels, local(): pl.pallas_call(finish, out_shape=(jax.ShapeDtypeStruct((1, VARS, LEV, CEL...  2.09 us

profile of v6, /device:TPU:1, one launch (start us, length us, event | category | flops | bytes accessed | tf_op | source)
XLA Modules:
  0.0 35.4 jit_solution(11991498934841319463)
XLA Ops:
  0.6 32.6 %step.1 = (f32[4,16,4096]{2,1,0:T(8,128)}, f32[4,4096]{1,0:T(4,128)}) custom-call(f32[1,4,16,4096]{3,2,1,0:T(8,128)} %state_hbm.1, s32[1,8,4096]{2,1,0:T(8,128)} %neighbours_hbm.1, f32[1,8,4096]{2,1,0:T(8,128)} %coef_hbm.1, f32[1,16,16]{2,1,0:T(8,128)} %mixing_hbm.3, s32[1,1,64]{2,1,0:T(1,128)} %count_hbm.1, s32[1,1,64,1024]{3,2,1,0:T(8,128)} %source_hbm.1, ...), custom_call_target="tpu_custom_call" | custom-call | tf_op jit(solution)/shard_map/step/pallas_call | solution.py:497
  33.3 2.1 %finish.1 = (f32[1,4,16,4096]{3,2,1,0:T(8,128)}, f32[1,4,4096]{2,1,0:T(4,128)}) custom-call(f32[4,16,4096]{2,1,0:T(8,128)} %get-tuple-element.4.mixed_hbm, f32[4,4096]{1,0:T(4,128)} %get-tuple-element.5.flux_in, f32[1,16,16]{2,1,0:T(8,128)} %mixing_hbm.3), custom_call_target="tpu_custom_call" | custom-call | tf_op jit(solution)/shard_map/finish/pallas_call | solution.py:547

commit v7 on v6

--- a/solution.py
+++ b/solution.py
@@ -23,7 +23,7 @@
 SPAN = 2 * HALO // LANES + 1
 BATCH = 16
 SENT = 8
-STENCIL_UNROLL = 4
+STENCIL_UNROLL = 8
 PRODUCTS = 4
 FROM_LEFT, FROM_RIGHT = 0, HALO + CELLS
 
@@ -312,7 +312,7 @@
             split[at, LANES : 2 * LANES] = low[:, e * LANES : (e + 1) * LANES]
         return c_
 
-    lax.fori_loop(0, (BLOCKS + SPAN - 1) // 4, blend, 0, unroll=3)
+    lax.fori_loop(0, (BLOCKS + SPAN - 1) // 4, blend, 0, unroll=9)
     for one_load in stencil_loads:
         one_load.wait()
 

time: 35.5 us -> 34.6 us (0.975)
  Pallas kernels: 34.7 us -> 33.7 us
    pallas_call x1, Pallas kernels: 32.6 us -> 31.7 us  [local(): pl.pallas_call(kernel, out_shape=(jax.ShapeDtypeStruct((VARS, LEV, CELLS)...]
where the time goes in v7:
time: 34.6 us; the launch traced here: 34.4 us
  Pallas kernels  33.7 us (97%)
  between operations  0.64 us (2%)
    pallas_call x1, Pallas kernels, local(): pl.pallas_call(kernel, out_shape=(jax.ShapeDtypeStruct((VARS, LEV, CELLS)...  31.7 us
    pallas_call x1, Pallas kernels, local(): pl.pallas_call(finish, out_shape=(jax.ShapeDtypeStruct((1, VARS, LEV, CEL...  2.09 us

profile of v7, /device:TPU:1, one launch (start us, length us, event | category | flops | bytes accessed | tf_op | source)
XLA Modules:
  0.0 34.4 jit_solution(13819486522353578845)
XLA Ops:
  0.6 31.7 %step.1 = (f32[4,16,4096]{2,1,0:T(8,128)}, f32[4,4096]{1,0:T(4,128)}) custom-call(f32[1,4,16,4096]{3,2,1,0:T(8,128)} %state_hbm.1, s32[1,8,4096]{2,1,0:T(8,128)} %neighbours_hbm.1, f32[1,8,4096]{2,1,0:T(8,128)} %coef_hbm.1, f32[1,16,16]{2,1,0:T(8,128)} %mixing_hbm.3, s32[1,1,64]{2,1,0:T(1,128)} %count_hbm.1, s32[1,1,64,1024]{3,2,1,0:T(8,128)} %source_hbm.1, ...), custom_call_target="tpu_custom_call" | custom-call | tf_op jit(solution)/shard_map/step/pallas_call | solution.py:497
  32.3 2.1 %finish.1 = (f32[1,4,16,4096]{3,2,1,0:T(8,128)}, f32[1,4,4096]{2,1,0:T(4,128)}) custom-call(f32[4,16,4096]{2,1,0:T(8,128)} %get-tuple-element.4.mixed_hbm, f32[4,4096]{1,0:T(4,128)} %get-tuple-element.5.flux_in, f32[1,16,16]{2,1,0:T(8,128)} %mixing_hbm.3), custom_call_target="tpu_custom_call" | custom-call | tf_op jit(solution)/shard_map/finish/pallas_call | solution.py:547
